TPU v7x, 32 devices: a whole 2x2x4 slice. The times are simulated.
32 devices in a mesh: grp: 2 (over y), inst: 4 (over x, core), tp: 4 (over z).
Axes of the slice: x: 2, y: 2, z: 4, core: 2. Of those that a mesh axis runs over, the one named last changes fastest.
Arguments:
- kv_pool: bfloat16 [8, 512, 8, 16, 256], P(('grp', 'inst'), None, 'tp'), parts along dimension 0, may hold values from -6 to 6, as said below
- block_table: int32 [8, 16, 32], P(('grp', 'inst')), parts along dimension 0, may hold values from 0 to 511, as said below
- lengths: int32 [8, 16], P('grp'), parts along dimension 0, may hold values from 0 to 512, as said below
- pairs: int32 [4, 2], P('grp'), parts along dimension 0, may hold values from 0 to 3, as said below
- moved: int32 [4, 2], P('grp'), parts along dimension 0, may hold values from 0 to 15, as said below
- queries: bfloat16 [2, 128, 8192], P(None, ('grp', 'inst'), 'tp'), parts along dimension 1, may hold values from -200 to 200
- fresh_kv: bfloat16 [2, 128, 2048], P(None, ('grp', 'inst'), 'tp'), parts along dimension 1, may hold values from -6 to 6, as said below
- out_weight: bfloat16 [8192, 8192], P('tp'), may hold values from -0.0625 to 0.0625
Outputs:
- layer_out: bfloat16 [2, 128, 8192], P(None, ('grp', 'inst'), 'tp'), parts along dimension 1
There are 2 independent parts, one for each index of `grp`. A program takes and returns all parts, laid end to end along the dimension named above; an argument that names none is the same for every part. Nothing has to cross between parts.
Inputs may be any that keep to these rules, and one draw needn't show every extreme that they name: `pairs`: each instance stands in at most one pair. `moved`: the slots of one pair are distinct. `lengths`: slots moved[p, :] hold 0 at instance pairs[p, 1]; every other slot holds 1 or more; moved[p, 0] holds 512 at instance pairs[p, 0]. `block_table`: each instance's table names each of its 512 blocks once. `kv_pool`: slots j and j' of the third dimension are equal where j = j'. `fresh_kv`: slots j and j' are equal where j = j'.
All inputs are finite; a program needn't handle non-finite values.
Results may differ from a plain program's by a relative error of at most 0.0058.
Values may be sent and summed in bfloat16 or wider, within the bound.
A program may use at most 128 MiB of HBM per device.

v0:
```python
import math

import jax
import jax.numpy as jnp
from jax import lax
from jax.sharding import PartitionSpec as P


def attend(query_rows, fresh_rows, cache, lens):
    steps, count, width = query_rows.shape
    groups = cache.shape[1]
    span = cache.shape[2]
    head_dim = cache.shape[3] // 2
    heads = width // head_dim
    scale = 1.0 / math.sqrt(head_dim)
    split_q = query_rows.reshape(steps, count, groups, heads // groups, head_dim)
    split_f = fresh_rows.reshape(steps, count, groups, 2 * head_dim)
    s_cache = (
        jnp.einsum(
            "trgqd,rgcd->trgqc", split_q, cache[..., :head_dim], preferred_element_type=jnp.float32
        )
        * scale
    )
    pos_ok = jnp.arange(span)[None, :] < lens[:, None]
    s_cache = jnp.where(pos_ok[None, :, None, None, :], s_cache, -1e30)
    s_new = (
        jnp.einsum(
            "trgqd,urgd->trgqu",
            split_q,
            split_f[..., :head_dim],
            preferred_element_type=jnp.float32,
        )
        * scale
    )
    step_ok = jnp.arange(steps)[None, :] <= jnp.arange(steps)[:, None]
    s_new = jnp.where(step_ok[:, None, None, None, :], s_new, -1e30)
    scores = jnp.concatenate([s_cache, s_new], axis=-1)
    top = jnp.max(scores, axis=-1, keepdims=True)
    expo = jnp.exp(scores - top)
    weights = (expo / jnp.sum(expo, axis=-1, keepdims=True)).astype(jnp.bfloat16)
    out = jnp.einsum(
        "trgqc,rgcd->trgqd",
        weights[..., :span],
        cache[..., head_dim:],
        preferred_element_type=jnp.float32,
    )
    out = out + jnp.einsum(
        "trgqu,urgd->trgqd",
        weights[..., span:],
        split_f[..., head_dim:],
        preferred_element_type=jnp.float32,
    )
    return out.astype(jnp.bfloat16).reshape(steps, count, width)


def on_device(kv_pool, block_table, lengths, pairs, moved, queries, fresh_kv, out_weight):
    pool = kv_pool[0]
    table = block_table[0]
    slots_here, blocks_each = table.shape
    groups = pool.shape[1]
    span = blocks_each * pool.shape[2]
    per_pair = moved.shape[1]
    steps = queries.shape[0]
    me = lax.axis_index("inst")
    slot_ids = jnp.arange(slots_here, dtype=jnp.int32)
    source_hit = pairs[:, 0] == me
    target_hit = pairs[:, 1] == me
    is_source = jnp.any(source_hit)
    is_target = jnp.any(target_hit)
    out_slots = jnp.sum(jnp.where(source_hit[:, None], moved, 0), axis=0)
    in_slots = jnp.sum(jnp.where(target_hit[:, None], moved, 0), axis=0)
    partner_src = jnp.sum(jnp.where(target_hit, pairs[:, 0], 0))
    own_lens = lengths[me]
    cache = pool[table].transpose(0, 2, 1, 3, 4).reshape(slots_here, groups, span, pool.shape[3])
    leaving = jnp.any(out_slots[:, None] == slot_ids[None, :], axis=0) & is_source
    payload = cache[out_slots]
    payload = jnp.where(is_source, payload, jnp.zeros_like(payload))
    arrived = lax.all_gather(payload, "inst", axis=0, tiled=True)
    chosen = lax.dynamic_slice_in_dim(arrived, partner_src * per_pair, per_pair, 0)
    cache = cache.at[in_slots].set(jnp.where(is_target, chosen, cache[in_slots]))
    lens = own_lens.at[in_slots].set(
        jnp.where(is_target, lengths[partner_src, in_slots], own_lens[in_slots])
    )
    attention = attend(queries, fresh_kv, cache, lens)
    attention = jnp.where(leaving[None, :, None], jnp.zeros_like(attention), attention)
    terms = jnp.dot(
        attention.reshape(steps * slots_here, attention.shape[2]),
        out_weight,
        preferred_element_type=jnp.float32,
    )
    shares = lax.psum_scatter(terms, "tp", scatter_dimension=1, tiled=True)
    return shares.astype(jnp.bfloat16).reshape(steps, slots_here, shares.shape[1])


def solution(mesh):
    in_specs = (
        P(("grp", "inst"), None, "tp", None, None),
        P(("grp", "inst"), None, None),
        P("grp", None),
        P("grp", None),
        P("grp", None),
        P(None, ("grp", "inst"), "tp"),
        P(None, ("grp", "inst"), "tp"),
        P("tp", None),
    )
    out_specs = P(None, ("grp", "inst"), "tp")
    return jax.shard_map(
        on_device, mesh=mesh, in_specs=in_specs, out_specs=out_specs, check_vma=False
    )
```

profile of v0, /device:TPU:0, one launch (start us, length us, event | category | flops | bytes accessed | tf_op | source)
XLA Modules:
  0.0 143.8 jit_solution(9102619001371971296)
XLA Ops:
  6.5 0.0 copy-start
  6.5 0.0 all-gather.2.cloned.1.call-start
  6.5 0.8 fusion.26
  7.4 0.1 copy.86
  7.5 0.1 copy.87
  7.6 0.7 compare_select_fusion
  8.2 0.1 reshape.124
  8.3 23.0 %gather_fusion = bf16[512,2,16,256]{3,2,1,0:T(8,128)(2,1)} fusion(bf16[512,2,16,256]{3,2,1,0:T(8,128)(2,1)} %bitcast.84, s32[1024]{0:T(1024)S(1)} %pad_clamp_fusion.2), kind=kCustom, calls=%fused_computation | custom fusion | bytes 16779264 | tf_op jit(solution)/shard_map/gather | solution.py:74
  31.4 0.0 copy-start.5
  31.4 7.8 %copy.70 = bf16[16,32,2,16,256]{4,3,1,2,0:T(8,128)(2,1)} copy(bf16[16,32,2,16,256]{4,3,2,1,0:T(8,128)(2,1)} %bitcast.80) | data formatting | bytes 16777216 | tf_op jit(solution)/shard_map/gather | solution.py:74
  39.2 0.6 compare_reduce_fusion.1
  39.8 0.0 copy-done.5
  39.8 0.1 select_reduce_fusion.1
  39.9 4.0 %gather_fusion.1 = bf16[2,2,512,256]{3,2,1,0:T(8,128)(2,1)S(1)} fusion(bf16[16,2,512,256]{3,2,1,0:T(8,128)(2,1)} %bitcast.81, s32[1024]{0:T(1024)S(1)} %pad_clamp_fusion.1), kind=kCustom, calls=%fused_computation.1 | custom fusion | bytes 2097160 | tf_op jit(solution)/shard_map/gather | solution.py:76
  43.9 1.7 %broadcast_select_fusion = bf16[2,2,512,256]{3,2,1,0:T(8,128)(2,1)} fusion(bf16[2,2,512,256]{3,2,1,0:T(8,128)(2,1)S(1)} %gather_fusion.1, pred[]{:T(512)} %get-tuple-element.17), kind=kLoop, calls=%fused_computation.22 | loop fusion | flops 524288 | bytes 2097153 | tf_op jit(solution)/shard_map/jit(_where)/select_n | solution.py:77
  45.6 0.0 all-gather.2.cloned.1.call-update
  45.6 0.0 reduce-scatter.2.cloned.1.call-start
  45.7 0.6 select_reduce_fusion.2
  48.3 4.0 %gather_fusion.2 = bf16[2,2,512,256]{3,2,1,0:T(8,128)(2,1)S(1)} fusion(bf16[16,2,512,256]{3,2,1,0:T(8,128)(2,1)} %bitcast.82, s32[1024]{0:T(1024)S(1)} %pad_clamp_fusion), kind=kCustom, calls=%fused_computation.2 | custom fusion | bytes 2097160 | tf_op jit(solution)/shard_map/gather | solution.py:80
  53.0 0.6 gather_fusion.4
  53.6 0.6 gather_fusion.3
  54.3 0.6 broadcast_select_fusion.1
  54.8 0.8 scatter_fusion.1
  55.6 0.0 copy-done.3
  55.7 0.7 fusion.15
  56.4 0.1 copy.75
  56.5 0.1 fusion.24
  56.6 0.1 copy.77
  56.7 0.4 copy.76
  57.0 0.1 compare_reduce_fusion
  57.1 0.6 broadcast_and_fusion
  57.7 0.1 broadcast_in_dim.91
  57.8 0.1 iota_compare_fusion
  57.9 25.1 %all-gather.2.cloned.1.call-done = bf16[8,2,512,256]{3,2,1,0:T(8,128)(2,1)} async-done(((bf16[2,2,512,256]{3,2,1,0:T(8,128)(2,1)}), bf16[8,2,512,256]{3,2,1,0:T(8,128)(2,1)}) %all-gather.2.cloned.1.call-update) | async-done | bytes 4194320 | tf_op jit(solution)/shard_map/all_gather | solution.py:78
  83.0 2.0 %dynamic-slice_select_fusion = bf16[2,2,512,256]{3,2,1,0:T(8,128)(2,1)S(1)} fusion(bf16[2,2,512,256]{3,2,1,0:T(8,128)(2,1)S(1)} %gather_fusion.2, bf16[8,2,512,256]{3,2,1,0:T(8,128)(2,1)} %all-gather.2.cloned.1.call-done, s32[]{:T(128)S(6)} %select_n.102, pred[]{:T(512)} %get-tuple-element.22), kind=kLoop, calls=%fused_computation.21 | loop fusion | flops 524288 | bytes 3145733 | tf_op jit(solution)/shard_map/jit(_where)/select_n | solution.py:80
  85.0 2.8 %scatter_fusion = bf16[16,2,512,256]{3,2,1,0:T(8,128)(2,1)} fusion(bf16[16,2,512,256]{3,2,1,0:T(8,128)(2,1)} %bitcast.83, s32[2]{0:T(128)S(1)} %get-tuple-element.14, bf16[2,2,512,256]{3,2,1,0:T(8,128)(2,1)S(1)} %dynamic-slice_select_fusion), kind=kCustom, calls=%fused_computation.5 | custom fusion | bytes 3145736 | tf_op jit(solution)/shard_map/scatter | solution.py:80
  87.8 3.6 %fusion.27 = (f32[2,16,2,8]{3,0,2,1:T(2,128)S(1)}, f32[2,16,2,8,512]{4,3,0,2,1:T(8,128)S(1)}) fusion(bf16[2,16,2,8,128]{4,3,2,1,0:T(8,128)(2,1)S(1)} %bitcast.87, bf16[16,2,512,256]{3,2,1,0:T(8,128)(2,1)} %scatter_fusion, pred[16,512]{1,0:T(8,128)(4,1)S(1)} %iota_compare_fusion), kind=kOutput, calls=%fused_computation.63 | convolution fusion | flops 67894784 | bytes 5384192 | tf_op jit(solution)/shard_map/trgqd,rgcd->trgqc/dot_general | solution.py:19
  91.4 0.4 fusion.9
  91.9 0.3 divide_convert_fusion
  92.2 0.2 copy-done.2
  92.4 0.6 fusion.6
  93.1 0.2 fusion.8
  93.3 0.1 reshape.120
  93.3 0.0 copy-start.1
  93.4 14.6 %fusion.12 = f32[32,8192]{1,0:T(8,128)} fusion(bf16[2048,8192]{1,0:T(8,128)(2,1)} %param.15, bf16[32,2048]{1,0:T(8,128)(2,1)S(1)} %reshape.120, pred[32]{0:T(512)(128)(4,1)S(1)} %broadcast_in_dim.91), kind=kOutput, calls=%fused_computation.26 | convolution fusion | flops 1073807360 | bytes 34734112 | tf_op jit(solution)/shard_map/dot_general | solution.py:86
  108.0 0.0 reduce-scatter.2.cloned.1.call-update
  108.0 27.3 %reduce-scatter.2.cloned.1.call-done = f32[32,2048]{1,0:T(8,128)} async-done(((f32[32,8192]{1,0:T(8,128)}), f32[32,2048]{1,0:T(8,128)}) %reduce-scatter.2.cloned.1.call-update) | async-done | bytes 262160 | tf_op jit(solution)/shard_map/reduce_scatter | solution.py:91
  135.3 1.6 %convert_element_type.11 = bf16[32,2048]{1,0:T(8,128)(2,1)} convert(f32[32,2048]{1,0:T(8,128)} %reduce-scatter.2.cloned.1.call-done) | non-fusion elementwise | flops 65536 | bytes 393216 | tf_op jit(solution)/shard_map/convert_element_type | solution.py:92
  (19 shorter events, 0.2 us)
Async XLA Ops:
  6.5 46.4 %copy-start = (s32[4,16]{1,0:T(4,128)S(1)}, s32[4,16]{1,0:T(4,128)}, u32[]{:S(2)}) copy-start(s32[4,16]{1,0:T(4,128)} %param.10) | copy-start | bytes 772
  6.5 76.4 %all-gather.2.cloned.1.call-start = ((), (), s32[]{:S(2)}) async-start(), calls=%async_computation.1 | async-start | bytes 5242880 | tf_op jit(solution)/shard_map/all_gather | solution.py:78
  31.4 8.4 %copy-start.5 = (s32[2,2]{1,0:T(2,128)S(1)}, s32[2,2]{1,0:T(2,128)}, u32[]{:S(2)}) copy-start(s32[2,2]{1,0:T(2,128)} %param.12) | copy-start | bytes 52
  39.2 16.4 %copy-start.3 = (bf16[2,16,2048]{2,1,0:T(8,128)(2,1)S(1)}, bf16[2,16,2048]{2,1,0:T(8,128)(2,1)}, u32[]{:S(2)}) copy-start(bf16[2,16,2048]{2,1,0:T(8,128)(2,1)} %param.13) | copy-start | bytes 393220
  39.2 16.5 %copy-start.4 = (bf16[2,16,512]{2,1,0:T(8,128)(2,1)S(1)}, bf16[2,16,512]{2,1,0:T(8,128)(2,1)}, u32[]{:S(2)}) copy-start(bf16[2,16,512]{2,1,0:T(8,128)(2,1)} %param.14) | copy-start | bytes 98308
  45.6 89.6 %reduce-scatter.2.cloned.1.call-start = ((), (), s32[]{:S(2)}) async-start(), calls=%async_computation.2 | async-start | bytes 1310720 | tf_op jit(solution)/shard_map/reduce_scatter | solution.py:91
  87.8 4.6 %copy-start.2 = (bf16[16,2,512,256]{3,2,1,0:T(8,128)(2,1)S(1)}, bf16[16,2,512,256]{3,2,1,0:T(8,128)(2,1)}, u32[]{:S(2)}) copy-start(bf16[16,2,512,256]{3,2,1,0:T(8,128)(2,1)} %scatter_fusion) | copy-start | bytes 25165828
  93.3 43.6 %copy-start.1 = (s32[4,16]{1,0:T(4,128)S(1)}, s32[4,16]{1,0:T(4,128)}, u32[]{:S(2)}) copy-start(s32[4,16]{1,0:T(4,128)} %param.10) | copy-start | bytes 772
Sparse Core Ops, SparseCore 0:
  45.8 37.1 all-gather.1
  108.1 27.1 reduce-scatter.1
where the time goes:
time: 144 us
  waiting for transfers between devices  52.4 us (36%)
  local copies, waits for them, and re-layouts  45.8 us (32%)
  matrix products  19.7 us (14%)
  between operations  16.2 us (11%)
  other arithmetic  9.56 us (7%)
    gather x2, local copies, waits for them, and re-layouts, on_device(): pool[table].transpose(0, 2, 1, 3, 4)  30.8 us
    reduce_scatter x1, waiting for transfers between devices, on_device(): shares = lax.psum_scatter(terms, 'tp', scatter_dimension=1, tiled=True)  27.3 us
    all_gather x1, waiting for transfers between devices, on_device(): arrived = lax.all_gather(payload, 'inst', axis=0, tiled=True)  25.1 us
    dot_general x1, matrix products, on_device(): jnp.dot(attention.reshape(steps * slots_here, attention.shape[2]), out_we...  14.6 us
    gather x1, local copies, waits for them, and re-layouts, on_device(): payload = cache[out_slots]  4 us
    gather x1, local copies, waits for them, and re-layouts, on_device(): cache[in_slots]  4 us
    dot_general x1, matrix products, attend(): jnp.einsum('trgqd,rgcd->trgqc', split_q, cache[..., :head_dim], preferred...  3.64 us
  transfers between devices with their start and end apart: 2, of which 2 were waited for; matrix products, arithmetic and copies ran while one was open for 7% of the time, Pallas kernels for 0%

commit v1 on v0

v1 whole, which is shorter than its diff:
```python
import functools
import math

import jax
import jax.numpy as jnp
from jax import lax
from jax.experimental import pallas as pl
from jax.experimental.pallas import tpu as pltpu
from jax.sharding import PartitionSpec as P

MESH = pl.DeviceIdType.MESH
F32 = jnp.float32
BF16 = jnp.bfloat16
LANE = 128
SUB = 8
PIECE = 512
POOL_CUTS = 8
TOGETHER = 4


def kernel(
    n_inst,
    n_tp,
    table,
    lengths,
    pairs,
    moved,
    pool,
    queries,
    fresh,
    weight,
    out,
    pool_v,
    q_v,
    f_v,
    w_v,
    q32,
    f32,
    o32,
    ask,
    reply,
    attn,
    part_send,
    part_recv,
    own,
    pool_sem,
    in_sem,
    w_sem,
    ask_send,
    ask_recv,
    reply_send,
    reply_recv,
    part_ssem,
    part_rsem,
):
    steps, slots, width = q_v.shape
    n_blocks = table.shape[1]
    groups = pool_v.shape[1]
    block = pool_v.shape[2]
    span = n_blocks * block
    per_pair = moved.shape[1]
    n_pairs = pairs.shape[0]
    hpg = width // LANE // groups
    rows = steps * slots
    pieces = own.shape[0]
    scale = 1.0 / math.sqrt(LANE)
    trow = slots * SUB
    q_rows = steps * SUB
    me = lax.axis_index("inst")
    my_tp = lax.axis_index("tp")

    def inst_peer(d):
        return lax.rem(me + d, n_inst)

    def tp_peer(d):
        return lax.rem(my_tp + d, n_tp)

    q_copy = pltpu.make_async_copy(queries, q_v, in_sem.at[0])
    f_copy = pltpu.make_async_copy(fresh, f_v, in_sem.at[1])
    q_copy.start()
    f_copy.start()
    cut = pool_v.shape[0] // POOL_CUTS
    pool_copies = [
        pltpu.make_async_copy(
            pool.at[pl.ds(i * cut, cut)], pool_v.at[pl.ds(i * cut, cut)], pool_sem.at[i]
        )
        for i in range(POOL_CUTS)
    ]
    for c in pool_copies:
        c.start()

    barrier = pltpu.get_barrier_semaphore()
    for d in range(1, n_inst):
        pl.semaphore_signal(barrier, inc=1, device_id={"inst": inst_peer(d)}, device_id_type=MESH)
    for d in range(1, n_tp):
        pl.semaphore_signal(barrier, inc=1, device_id={"tp": tp_peer(d)}, device_id_type=MESH)

    zero = jnp.int32(0)
    is_source, is_target = zero, zero
    to_inst, from_inst = zero, zero
    out_slots = [zero] * per_pair
    in_slots = [zero] * per_pair
    for p in range(n_pairs):
        src = jnp.where(pairs[p, 0] == me, 1, 0)
        dst = jnp.where(pairs[p, 1] == me, 1, 0)
        is_source += src
        is_target += dst
        to_inst += src * pairs[p, 1]
        from_inst += dst * pairs[p, 0]
        for k in range(per_pair):
            out_slots[k] += src * moved[p, k]
            in_slots[k] += dst * moved[p, k]
    to_inst = jnp.where(is_source > 0, to_inst, me)
    from_inst = jnp.where(is_target > 0, from_inst, me)

    q32[...] = jnp.zeros_like(q32)
    f32[...] = jnp.zeros_like(f32)
    q_copy.wait()
    f_copy.wait()
    qs = q_v[...].astype(F32).reshape(rows, width)
    for g in range(groups):
        for h in range(hpg):
            c0 = (g * hpg + h) * LANE
            q32[g, pl.ds(h, rows, stride=SUB), :] = qs[:, c0 : c0 + LANE]
    for u in range(steps):
        row = f_v[u].astype(F32)
        for c in range(2 * groups):
            f32[c, pl.ds(u, slots, stride=SUB), :] = row[:, c * LANE : (c + 1) * LANE]

    def q_of(g, s):
        at = pl.multiple_of(s * SUB, SUB)
        return jnp.concatenate(
            [q32[g, pl.ds(t * trow + at, SUB), :] for t in range(steps)], axis=0
        ).astype(BF16)

    mine = n_inst - 1
    base_q = per_pair * groups
    masks = [
        [jnp.full((SUB, LANE), in_slots[k], jnp.int32) == s for s in range(slots)]
        for k in range(per_pair)
    ]

    def pick(k, load):
        val = load(0)
        for s in range(1, slots):
            val = jnp.where(masks[k][s], load(s), val)
        return val

    for k in range(per_pair):
        for g in range(groups):
            ask[mine, k * groups + g] = jnp.concatenate(
                [
                    pick(k, lambda s: q32[g, pl.ds(t * trow + s * SUB, SUB), :])
                    for t in range(steps)
                ],
                axis=0,
            ).astype(BF16)
    for c in range(2 * groups):
        ask[mine, base_q + c] = jnp.concatenate(
            [pick(k, lambda s: f32[c, pl.ds(s * SUB, SUB), :]) for k in range(per_pair)], axis=0
        ).astype(BF16)

    pl.semaphore_wait(barrier, n_inst + n_tp - 2)

    asks = [
        pltpu.make_async_remote_copy(
            src_ref=ask.at[mine],
            dst_ref=ask.at[d - 1],
            send_sem=ask_send.at[d - 1],
            recv_sem=ask_recv.at[d - 1],
            device_id={"inst": inst_peer(d)},
            device_id_type=MESH,
        )
        for d in range(1, n_inst)
    ]
    for c in asks:
        c.start()

    for c in pool_copies:
        c.wait()

    order = list(range(1, n_tp)) + [0]
    w_copies = {}
    for d in order:
        for i in range(pieces):
            n = d * pieces + i
            col = pl.multiple_of(tp_peer(d) * (pieces * PIECE) + i * PIECE, PIECE)
            w_copies[d, i] = pltpu.make_async_copy(
                weight.at[:, pl.ds(col, PIECE)], w_v.at[n], w_sem.at[n]
            )
            w_copies[d, i].start()

    pos = lax.broadcasted_iota(jnp.int32, (groups * q_rows, span), 1)
    new_col = lax.broadcasted_iota(jnp.int32, (groups * q_rows, 2 * SUB), 1)
    new_step = lax.rem(
        lax.broadcasted_iota(jnp.int32, (groups * q_rows, 2 * SUB), 0), q_rows
    ) // SUB
    nt = (((1,), (1,)), ((), ()))

    def attend(q_groups, fresh_tiles, base, slot, length):
        wide = []
        for g in range(groups):
            line = [jnp.zeros((q_rows, LANE), BF16)] * groups
            line[g] = q_groups[g]
            wide.append(jnp.concatenate(line, axis=1))
        q = jnp.concatenate(wide, axis=0)
        keys, vals = [], []
        for j in range(n_blocks):
            b = table[slot, j]
            keys.append(jnp.concatenate([pool_v[b, g, :, :LANE] for g in range(groups)], axis=1))
            vals.append(jnp.concatenate([pool_v[b, g, :, LANE:] for g in range(groups)], axis=1))
        keys = jnp.concatenate(keys, axis=0)
        vals = jnp.concatenate(vals, axis=0)
        k_new = jnp.concatenate([fresh_tiles[2 * g] for g in range(groups)], axis=1)
        v_new = jnp.concatenate([fresh_tiles[2 * g + 1] for g in range(groups)], axis=1)
        s_old = lax.dot_general(q, keys, nt, preferred_element_type=F32) * scale
        s_new = lax.dot_general(q, k_new, nt, preferred_element_type=F32) * scale
        s_old = jnp.where(pos < length, s_old, -1e30)
        ok = (new_col >= base) & (new_col <= new_step + base)
        s_new = jnp.where(ok, s_new, -1e30)
        top = jnp.maximum(
            jnp.max(s_old, axis=1, keepdims=True), jnp.max(s_new, axis=1, keepdims=True)
        )
        e_old = jnp.exp(s_old - top)
        e_new = jnp.exp(s_new - top)
        total = jnp.sum(e_old, axis=1, keepdims=True) + jnp.sum(e_new, axis=1, keepdims=True)
        inv = 1.0 / total
        p_old = (e_old * inv).astype(BF16)
        p_new = (e_new * inv).astype(BF16)
        o = jnp.dot(p_old, vals, preferred_element_type=F32)
        o = o + jnp.dot(p_new, v_new, preferred_element_type=F32)
        return [
            o[g * q_rows : (g + 1) * q_rows, g * LANE : (g + 1) * LANE].astype(BF16)
            for g in range(groups)
        ]

    def own_slots(first, count):
        @pl.loop(0, count // TOGETHER)
        def _(it):
            for e in range(TOGETHER):
                s = first + it * TOGETHER + e
                pair_at = pl.multiple_of((s // 2) * (2 * SUB), 2 * SUB)
                tiles = [f32[c, pl.ds(pair_at, 2 * SUB), :].astype(BF16) for c in range(2 * groups)]
                res = attend(
                    [q_of(g, s) for g in range(groups)],
                    tiles,
                    lax.rem(s, 2) * SUB,
                    s,
                    lengths[me, s],
                )
                at = pl.multiple_of(s * SUB, SUB)
                for g in range(groups):
                    r = res[g].astype(F32)
                    for t in range(steps):
                        o32[g, pl.ds(t * trow + at, SUB), :] = r[t * SUB : (t + 1) * SUB]

    half = slots // 2
    own_slots(0, half)

    for c in asks:
        c.wait_recv()
    asker = lax.rem(me - to_inst + 2 * n_inst - 1, n_inst)
    for k in range(per_pair):
        res = attend(
            [ask[asker, k * groups + g] for g in range(groups)],
            [ask[asker, base_q + c] for c in range(2 * groups)],
            k * SUB,
            out_slots[k],
            lengths[me, out_slots[k]],
        )
        for g in range(groups):
            reply[mine, k * groups + g] = res[g]
    replies = [
        pltpu.make_async_remote_copy(
            src_ref=reply.at[mine],
            dst_ref=reply.at[d - 1],
            send_sem=reply_send.at[d - 1],
            recv_sem=reply_recv.at[d - 1],
            device_id={"inst": inst_peer(d)},
            device_id_type=MESH,
        )
        for d in range(1, n_inst)
    ]
    for c in replies:
        c.start()

    own_slots(half, slots - half)

    for c in replies:
        c.wait_recv()
    answer = lax.rem(me - from_inst + 2 * n_inst - 1, n_inst)
    for g in range(groups):
        got = [reply[answer, k * groups + g].astype(F32) for k in range(per_pair)]
        for s in range(slots):
            for t in range(steps):
                r0 = t * trow + s * SUB
                val = o32[g, r0 : r0 + SUB, :]
                for k in range(per_pair):
                    at = jnp.where(is_target > 0, in_slots[k], -1)
                    hit = jnp.full((SUB, LANE), at, jnp.int32) == s
                    val = jnp.where(hit, got[k][t * SUB : (t + 1) * SUB], val)
                for k in range(per_pair):
                    at = jnp.where(is_source > 0, out_slots[k], -1)
                    hit = jnp.full((SUB, LANE), at, jnp.int32) == s
                    val = jnp.where(hit, 0.0, val)
                o32[g, r0 : r0 + SUB, :] = val
    for g in range(groups):
        for h in range(hpg):
            c0 = (g * hpg + h) * LANE
            attn[:, c0 : c0 + LANE] = o32[g, pl.ds(h, rows, stride=SUB), :].astype(BF16)

    sends = []
    for d in order:
        for i in range(pieces):
            w_copies[d, i].wait()
            part = jnp.dot(attn[...], w_v[d * pieces + i], preferred_element_type=F32)
            if d == 0:
                own[i] = part
            else:
                part_send[d - 1, i] = part.astype(BF16)
                c = pltpu.make_async_remote_copy(
                    src_ref=part_send.at[d - 1, i],
                    dst_ref=part_recv.at[d - 1, i],
                    send_sem=part_ssem.at[d - 1, i],
                    recv_sem=part_rsem.at[d - 1, i],
                    device_id={"tp": tp_peer(d)},
                    device_id_type=MESH,
                )
                c.start()
                sends.append(c)
    for c in sends:
        c.wait_recv()
    for i in range(pieces):
        total = own[i]
        for d in range(1, n_tp):
            total = total + part_recv[d - 1, i].astype(F32)
        out[:, i * PIECE : (i + 1) * PIECE] = total.astype(BF16)
    for c in asks + replies + sends:
        c.wait_send()


def on_device(n_inst, n_tp, kv_pool, block_table, lengths, pairs, moved, queries, fresh_kv, out_weight):
    pool = kv_pool[0]
    table = block_table[0]
    slots, n_blocks = table.shape
    n_pool, groups, block, wide = pool.shape
    steps, _, width = queries.shape
    per_pair = moved.shape[1]
    rows = steps * slots
    d_model = out_weight.shape[1]
    cols = d_model // n_tp
    pieces = cols // PIECE
    tiles = per_pair * groups + 2 * groups
    vm = pltpu.VMEM
    dma = pltpu.SemaphoreType.DMA
    smem = pl.BlockSpec(memory_space=pltpu.SMEM)
    hbm = pl.BlockSpec(memory_space=pl.ANY)
    out = pl.pallas_call(
        functools.partial(kernel, n_inst, n_tp),
        out_shape=jax.ShapeDtypeStruct((rows, cols), BF16),
        in_specs=[smem] * 4 + [hbm] * 4,
        out_specs=pl.BlockSpec(memory_space=pltpu.VMEM),
        scratch_shapes=[
            vm(pool.shape, BF16),
            vm(queries.shape, BF16),
            vm(fresh_kv.shape, BF16),
            vm((n_tp * pieces, width, PIECE), BF16),
            vm((groups, rows * SUB, LANE), F32),
            vm((2 * groups, slots * SUB, LANE), F32),
            vm((groups, rows * SUB, LANE), F32),
            vm((n_inst, tiles, 2 * SUB, LANE), BF16),
            vm((n_inst, per_pair * groups, 2 * SUB, LANE), BF16),
            vm((rows, width), BF16),
            vm((n_tp - 1, pieces, rows, PIECE), BF16),
            vm((n_tp - 1, pieces, rows, PIECE), BF16),
            vm((pieces, rows, PIECE), F32),
            dma((POOL_CUTS,)),
            dma((2,)),
            dma((n_tp * pieces,)),
            dma((n_inst - 1,)),
            dma((n_inst - 1,)),
            dma((n_inst - 1,)),
            dma((n_inst - 1,)),
            dma((n_tp - 1, pieces)),
            dma((n_tp - 1, pieces)),
        ],
        compiler_params=pltpu.CompilerParams(
            collective_id=0, has_side_effects=True, vmem_limit_bytes=56 * 2**20
        ),
        cost_estimate=pl.CostEstimate(
            flops=2 * rows * width * d_model,
            bytes_accessed=2 * (width * d_model + pool.size),
            transcendentals=0,
        ),
    )(table, lengths, pairs, moved, pool, queries, fresh_kv, out_weight)
    return out.reshape(steps, slots, cols)


def solution(mesh):
    in_specs = (
        P(("grp", "inst"), None, "tp", None, None),
        P(("grp", "inst"), None, None),
        P("grp", None),
        P("grp", None),
        P("grp", None),
        P(None, ("grp", "inst"), "tp"),
        P(None, ("grp", "inst"), "tp"),
        P("tp", None),
    )
    out_specs = P(None, ("grp", "inst"), "tp")
    body = functools.partial(on_device, mesh.shape["inst"], mesh.shape["tp"])
    return jax.shard_map(body, mesh=mesh, in_specs=in_specs, out_specs=out_specs, check_vma=False)
```

time: 144 us -> 31.5 us (0.22)
  the two profiles are of different devices: /device:TPU:0 before, /device:TPU:9 now
where the time goes in v1:
time: 31.5 us; the launch traced here: 31.3 us
  Pallas kernels  29.8 us (95%)
  local copies, waits for them, and re-layouts  1.57 us (5%)
    pallas_call x1, Pallas kernels, on_device(): pl.pallas_call(functools.partial(kernel, n_inst, n_tp), out_shape=jax.Sha...  29.8 us
    unnamed x1, local copies, waits for them, and re-layouts  1.57 us

profile of v1, /device:TPU:9, one launch (start us, length us, event | category | flops | bytes accessed | tf_op | source)
XLA Modules:
  0.0 31.3 jit_solution(10740185891951186783)
XLA Ops:
  0.0 29.8 %shard_map.82 = bf16[32,2048]{1,0:T(8,128)(2,1)} custom-call(s32[16,32]{1,0:T(8,128)} %bitcast.5, s32[4,16]{1,0:T(4,128)} %lengths.1, s32[2,2]{1,0:T(2,128)} %pairs.1, s32[2,2]{1,0:T(2,128)} %moved.1, bf16[512,2,16,256]{3,2,1,0:T(8,128)(2,1)} %bitcast.3, bf16[2,16,2048]{2,1,0:T(8,128)(2,1)} %queries.1, bf16[2,16,512]{2,1,0:T(8,128)(2,1)} %fresh.1, ...), custom_call_target="tpu_custom_call" | custom-call | flops 1073741824 | bytes 41943040 | tf_op jit(solution)/shard_map/pallas_call | solution.py:358
  29.8 1.6 %copy.10 = bf16[2,16,2048]{2,1,0:T(8,128)(2,1)} copy(bf16[2,16,2048]{2,1,0:T(8,128)(2,1)} %bitcast.4) | data formatting | bytes 262144

commit v2 on v1

--- a/solution.py
+++ b/solution.py
@@ -88,6 +88,15 @@
     ]
     for c in pool_copies:
         c.start()
+    order = [(d, i) for i in range(pieces) for d in list(range(1, n_tp)) + [0]]
+    w_copies = {}
+    for d, i in order:
+        n = d * pieces + i
+        col = pl.multiple_of(tp_peer(d) * (pieces * PIECE) + i * PIECE, PIECE)
+        w_copies[d, i] = pltpu.make_async_copy(
+            weight.at[:, pl.ds(col, PIECE)], w_v.at[n], w_sem.at[n]
+        )
+        w_copies[d, i].start()
 
     barrier = pltpu.get_barrier_semaphore()
     for d in range(1, n_inst):
@@ -178,17 +187,6 @@
 
     for c in pool_copies:
         c.wait()
-
-    order = list(range(1, n_tp)) + [0]
-    w_copies = {}
-    for d in order:
-        for i in range(pieces):
-            n = d * pieces + i
-            col = pl.multiple_of(tp_peer(d) * (pieces * PIECE) + i * PIECE, PIECE)
-            w_copies[d, i] = pltpu.make_async_copy(
-                weight.at[:, pl.ds(col, PIECE)], w_v.at[n], w_sem.at[n]
-            )
-            w_copies[d, i].start()
 
     pos = lax.broadcasted_iota(jnp.int32, (groups * q_rows, span), 1)
     new_col = lax.broadcasted_iota(jnp.int32, (groups * q_rows, 2 * SUB), 1)
@@ -254,22 +252,75 @@
                     for t in range(steps):
                         o32[g, pl.ds(t * trow + at, SUB), :] = r[t * SUB : (t + 1) * SUB]
 
-    half = slots // 2
-    own_slots(0, half)
+    own_slots(0, slots)
 
     for c in asks:
         c.wait_recv()
     asker = lax.rem(me - to_inst + 2 * n_inst - 1, n_inst)
-    for k in range(per_pair):
-        res = attend(
+    away = [jnp.where(is_source > 0, out_slots[k], -1) for k in range(per_pair)]
+    here = [jnp.where(is_target > 0, in_slots[k], -1) for k in range(per_pair)]
+    got = [
+        attend(
             [ask[asker, k * groups + g] for g in range(groups)],
             [ask[asker, base_q + c] for c in range(2 * groups)],
             k * SUB,
             out_slots[k],
             lengths[me, out_slots[k]],
         )
+        for k in range(per_pair)
+    ]
+    for s in range(slots):
+        hits = [jnp.full((SUB, LANE), away[k], jnp.int32) == s for k in range(per_pair)]
         for g in range(groups):
-            reply[mine, k * groups + g] = res[g]
+            for t in range(steps):
+                r0 = t * trow + s * SUB
+                val = o32[g, r0 : r0 + SUB, :]
+                for k in range(per_pair):
+                    val = jnp.where(hits[k], got[k][g][t * SUB : (t + 1) * SUB].astype(F32), val)
+                o32[g, r0 : r0 + SUB, :] = val
+    for g in range(groups):
+        for h in range(hpg):
+            c0 = (g * hpg + h) * LANE
+            attn[:, c0 : c0 + LANE] = o32[g, pl.ds(h, rows, stride=SUB), :].astype(BF16)
+
+    sends = {}
+    for d, i in order:
+        w_copies[d, i].wait()
+        part = jnp.dot(attn[...], w_v[d * pieces + i], preferred_element_type=F32)
+        if d == 0:
+            own[i] = part
+        else:
+            part_send[d - 1, i] = part.astype(BF16)
+            c = pltpu.make_async_remote_copy(
+                src_ref=part_send.at[d - 1, i],
+                dst_ref=part_recv.at[d - 1, i],
+                send_sem=part_ssem.at[d - 1, i],
+                recv_sem=part_rsem.at[d - 1, i],
+                device_id={"tp": tp_peer(d)},
+                device_id_type=MESH,
+            )
+            c.start()
+            sends[d, i] = c
+
+    n_back = reply.shape[1]
+    b_row = lax.broadcasted_iota(jnp.int32, (n_back, rows), 0)
+    b_col = lax.broadcasted_iota(jnp.int32, (n_back, rows), 1)
+    back = jnp.zeros((n_back, PIECE), F32)
+    totals = []
+    for i in range(pieces):
+        total = own[i]
+        for d in range(1, n_tp):
+            sends[d, i].wait_recv()
+            total = total + part_recv[d - 1, i].astype(F32)
+        total = total.astype(BF16)
+        totals.append(total)
+        hot = jnp.zeros((n_back, rows), F32)
+        for k in range(per_pair):
+            for t in range(steps):
+                at = (i * per_pair + k) * steps + t
+                hot = jnp.where((b_row == at) & (b_col == out_slots[k] + t * slots), 1.0, hot)
+        back = back + jnp.dot(hot.astype(BF16), total, preferred_element_type=F32)
+    reply[mine] = back.astype(BF16)
     replies = [
         pltpu.make_async_remote_copy(
             src_ref=reply.at[mine],
@@ -283,59 +334,29 @@
     ]
     for c in replies:
         c.start()
-
-    own_slots(half, slots - half)
-
+    answer = lax.rem(me - from_inst + 2 * n_inst - 1, n_inst)
+    slot_of = lax.rem(lax.broadcasted_iota(jnp.int32, (rows, PIECE), 0), slots)
+    gone = slot_of == away[0]
+    come = slot_of == here[0]
+    for k in range(1, per_pair):
+        gone = gone | (slot_of == away[k])
+        come = come | (slot_of == here[k])
+    f_row = lax.broadcasted_iota(jnp.int32, (rows, n_back), 0)
+    f_col = lax.broadcasted_iota(jnp.int32, (rows, n_back), 1)
     for c in replies:
         c.wait_recv()
-    answer = lax.rem(me - from_inst + 2 * n_inst - 1, n_inst)
-    for g in range(groups):
-        got = [reply[answer, k * groups + g].astype(F32) for k in range(per_pair)]
-        for s in range(slots):
+    result = reply[answer]
+    for i in range(pieces):
+        hot = jnp.zeros((rows, n_back), F32)
+        for k in range(per_pair):
             for t in range(steps):
-                r0 = t * trow + s * SUB
-                val = o32[g, r0 : r0 + SUB, :]
-                for k in range(per_pair):
-                    at = jnp.where(is_target > 0, in_slots[k], -1)
-                    hit = jnp.full((SUB, LANE), at, jnp.int32) == s
-                    val = jnp.where(hit, got[k][t * SUB : (t + 1) * SUB], val)
-                for k in range(per_pair):
-                    at = jnp.where(is_source > 0, out_slots[k], -1)
-                    hit = jnp.full((SUB, LANE), at, jnp.int32) == s
-                    val = jnp.where(hit, 0.0, val)
-                o32[g, r0 : r0 + SUB, :] = val
-    for g in range(groups):
-        for h in range(hpg):
-            c0 = (g * hpg + h) * LANE
-            attn[:, c0 : c0 + LANE] = o32[g, pl.ds(h, rows, stride=SUB), :].astype(BF16)
-
-    sends = []
-    for d in order:
-        for i in range(pieces):
-            w_copies[d, i].wait()
-            part = jnp.dot(attn[...], w_v[d * pieces + i], preferred_element_type=F32)
-            if d == 0:
-                own[i] = part
-            else:
-                part_send[d - 1, i] = part.astype(BF16)
-                c = pltpu.make_async_remote_copy(
-                    src_ref=part_send.at[d - 1, i],
-                    dst_ref=part_recv.at[d - 1, i],
-                    send_sem=part_ssem.at[d - 1, i],
-                    recv_sem=part_rsem.at[d - 1, i],
-                    device_id={"tp": tp_peer(d)},
-                    device_id_type=MESH,
-                )
-                c.start()
-                sends.append(c)
-    for c in sends:
-        c.wait_recv()
-    for i in range(pieces):
-        total = own[i]
-        for d in range(1, n_tp):
-            total = total + part_recv[d - 1, i].astype(F32)
-        out[:, i * PIECE : (i + 1) * PIECE] = total.astype(BF16)
-    for c in asks + replies + sends:
+                at = (i * per_pair + k) * steps + t
+                hot = jnp.where((f_col == at) & (f_row == in_slots[k] + t * slots), 1.0, hot)
+        moved_in = jnp.dot(hot.astype(BF16), result, preferred_element_type=F32)
+        val = jnp.where(come, moved_in, totals[i].astype(F32))
+        val = jnp.where(gone, 0.0, val)
+        out[:, i * PIECE : (i + 1) * PIECE] = val.astype(BF16)
+    for c in asks + replies + list(sends.values()):
         c.wait_send()
 
 
@@ -351,6 +372,7 @@
     cols = d_model // n_tp
     pieces = cols // PIECE
     tiles = per_pair * groups + 2 * groups
+    back = -(-(pieces * per_pair * steps) // 16) * 16
     vm = pltpu.VMEM
     dma = pltpu.SemaphoreType.DMA
     smem = pl.BlockSpec(memory_space=pltpu.SMEM)
@@ -369,7 +391,7 @@
             vm((2 * groups, slots * SUB, LANE), F32),
             vm((groups, rows * SUB, LANE), F32),
             vm((n_inst, tiles, 2 * SUB, LANE), BF16),
-            vm((n_inst, per_pair * groups, 2 * SUB, LANE), BF16),
+            vm((n_inst, back, PIECE), BF16),
             vm((rows, width), BF16),
             vm((n_tp - 1, pieces, rows, PIECE), BF16),
             vm((n_tp - 1, pieces, rows, PIECE), BF16),

time: 31.5 us -> 45.4 us (1.44)
  the two profiles are of different devices: /device:TPU:9 before, /device:TPU:0 now
where the time goes in v2:
time: 45.4 us; the launch traced here: 45.2 us
  Pallas kernels  43.6 us (96%)
  local copies, waits for them, and re-layouts  1.57 us (3%)
    pallas_call x1, Pallas kernels, on_device(): pl.pallas_call(functools.partial(kernel, n_inst, n_tp), out_shape=jax.Sha...  43.6 us
    unnamed x1, local copies, waits for them, and re-layouts  1.57 us

profile of v2, /device:TPU:0, one launch (start us, length us, event | category | flops | bytes accessed | tf_op | source)
XLA Modules:
  0.0 45.2 jit_solution(5043772099458505986)
XLA Ops:
  0.0 43.6 %shard_map.82 = bf16[32,2048]{1,0:T(8,128)(2,1)} custom-call(s32[16,32]{1,0:T(8,128)} %bitcast.5, s32[4,16]{1,0:T(4,128)} %lengths.1, s32[2,2]{1,0:T(2,128)} %pairs.1, s32[2,2]{1,0:T(2,128)} %moved.1, bf16[512,2,16,256]{3,2,1,0:T(8,128)(2,1)} %bitcast.3, bf16[2,16,2048]{2,1,0:T(8,128)(2,1)} %queries.1, bf16[2,16,512]{2,1,0:T(8,128)(2,1)} %fresh.1, ...), custom_call_target="tpu_custom_call" | custom-call | flops 1073741824 | bytes 41943040 | tf_op jit(solution)/shard_map/pallas_call | solution.py:380
  43.6 1.6 %copy.10 = bf16[2,16,2048]{2,1,0:T(8,128)(2,1)} copy(bf16[2,16,2048]{2,1,0:T(8,128)(2,1)} %bitcast.4) | data formatting | bytes 262144

commit v3 on v1

--- a/solution.py
+++ b/solution.py
@@ -179,7 +179,8 @@
     for c in pool_copies:
         c.wait()
 
-    order = list(range(1, n_tp)) + [0]
+    middle = n_tp // 2
+    order = [middle] + [d for d in range(1, n_tp) if d != middle] + [0]
     w_copies = {}
     for d in order:
         for i in range(pieces):

time: 31.5 us -> 31.6 us (level)
  the two profiles are of different devices: /device:TPU:9 before, /device:TPU:0 now
where the time goes in v3:
time: 31.6 us; the launch traced here: 31.5 us
  Pallas kernels  29.9 us (95%)
  local copies, waits for them, and re-layouts  1.57 us (5%)
    pallas_call x1, Pallas kernels, on_device(): pl.pallas_call(functools.partial(kernel, n_inst, n_tp), out_shape=jax.Sha...  29.9 us
    unnamed x1, local copies, waits for them, and re-layouts  1.57 us

profile of v3, /device:TPU:0, one launch (start us, length us, event | category | flops | bytes accessed | tf_op | source)
XLA Modules:
  0.0 31.5 jit_solution(10794705809981284426)
XLA Ops:
  0.0 29.9 %shard_map.82 = bf16[32,2048]{1,0:T(8,128)(2,1)} custom-call(s32[16,32]{1,0:T(8,128)} %bitcast.5, s32[4,16]{1,0:T(4,128)} %lengths.1, s32[2,2]{1,0:T(2,128)} %pairs.1, s32[2,2]{1,0:T(2,128)} %moved.1, bf16[512,2,16,256]{3,2,1,0:T(8,128)(2,1)} %bitcast.3, bf16[2,16,2048]{2,1,0:T(8,128)(2,1)} %queries.1, bf16[2,16,512]{2,1,0:T(8,128)(2,1)} %fresh.1, ...), custom_call_target="tpu_custom_call" | custom-call | flops 1073741824 | bytes 41943040 | tf_op jit(solution)/shard_map/pallas_call | solution.py:359
  29.9 1.6 %copy.10 = bf16[2,16,2048]{2,1,0:T(8,128)(2,1)} copy(bf16[2,16,2048]{2,1,0:T(8,128)(2,1)} %bitcast.4) | data formatting | bytes 262144
